TPU v7x, 512 devices: a whole 4x4x16 slice. The times are simulated.
512 devices in a mesh: wide: 64 (over y, x, z_hi), narrow: 8 (over z_lo, core).
Axes of the slice: x: 4, y: 4, z: 16 (z_hi: 4, z_lo: 4; z = z_hi * 4 + z_lo), core: 2. Of those that a mesh axis runs over, the one named last changes fastest.
Arguments:
- star_state: float32 [12, 65536], P(None, ('wide', 'narrow')), may hold values from -6 to 6
- masses: float32 [65536], P(('wide', 'narrow')), may hold values from 0.1 to 10
- levels: int32 [65536], P(('wide', 'narrow')), may hold values from 0 to 3
- active: int32 [16384], replicated, may hold values from 0 to 65535, as said below
Outputs:
- updated: float32 [12, 49152], P(None, ('wide', 'narrow'))
Inputs may be any that keep to these rules, and one draw needn't show every extreme that they name: `active`: distinct and ascending; the stars i with the same i // 128 number at most 96, and exactly 96 for some such group in every draw.
All inputs are finite; a program needn't handle non-finite values.
Results may differ from a plain program's by a relative error of at most 0.00012.
Values sent between devices are 32-bit elements; how exact they have to be, the bound alone decides.
A program may use at most 128 MiB of HBM per device.

v0:
```python
import math

import jax
import jax.numpy as jnp
from jax import lax
from jax.sharding import PartitionSpec as P

CAP = 96


soft_sq = 0.01


def predict(star_state, levels):
    step_len = jnp.exp2(-levels.astype(star_state.dtype))
    position = star_state[0:3]
    velocity = star_state[3:6]
    accel = star_state[6:9]
    jerks = star_state[9:12]
    new_pos = position + step_len * (
        velocity + step_len * (accel * 0.5 + step_len * jerks * (1.0 / 6.0))
    )
    new_vel = velocity + step_len * (accel + step_len * jerks * 0.5)
    return jnp.concatenate([new_pos, new_vel], axis=0)


def correct(old_state, old_levels, fresh):
    step_len = jnp.exp2(-old_levels.astype(old_state.dtype))
    half_step = step_len * 0.5
    twelfth = step_len * step_len * (1.0 / 12.0)
    old_pos = old_state[0:3]
    old_vel = old_state[3:6]
    old_acc = old_state[6:9]
    old_jerk = old_state[9:12]
    new_acc = fresh[0:3]
    new_jerk = fresh[3:6]
    new_vel = old_vel + half_step * (old_acc + new_acc) + twelfth * (old_jerk - new_jerk)
    new_pos = old_pos + half_step * (old_vel + new_vel) + twelfth * (old_acc - new_acc)
    return jnp.concatenate([new_pos, new_vel, new_acc, new_jerk], axis=0)


def pull_block(targets, sources):
    sep = [sources[dim_idx][None, :] - targets[dim_idx][:, None] for dim_idx in range(3)]
    rel = [sources[dim_idx + 3][None, :] - targets[dim_idx + 3][:, None] for dim_idx in range(3)]
    dist_sq = sep[0] * sep[0] + sep[1] * sep[1] + sep[2] * sep[2] + soft_sq
    inverse_sq = 1.0 / dist_sq
    strength = sources[6][None, :] * jnp.sqrt(inverse_sq) * inverse_sq
    radial = 3.0 * (sep[0] * rel[0] + sep[1] * rel[1] + sep[2] * rel[2]) * inverse_sq
    accel = [jnp.sum(strength * sep[dim_idx], axis=1) for dim_idx in range(3)]
    jerks = [
        jnp.sum(strength * (rel[dim_idx] - radial * sep[dim_idx]), axis=1) for dim_idx in range(3)
    ]
    return jnp.stack(accel + jerks, axis=0)


def pull(targets, sources):
    howmany = targets.shape[1]
    tile_size = math.gcd(howmany, max(8, (1 << 18) // sources.shape[1]))
    grouped = targets.reshape(6, howmany // tile_size, tile_size).transpose(1, 0, 2)
    results = lax.map(lambda tile_block: pull_block(tile_block, sources), grouped)
    return results.transpose(1, 0, 2).reshape(6, howmany)


def on_device(star_state, masses, levels, active):
    local_count = star_state.shape[1]
    owners = lax.axis_size(("wide", "narrow"))
    myself = lax.axis_index(("wide", "narrow"))
    grav = 1.0 / (local_count * owners)
    predicted = predict(star_state, levels)
    sources = jnp.concatenate([predicted, (masses * grav)[None, :]], axis=0)
    base_index = myself * local_count
    run_begin = jnp.searchsorted(active, base_index)
    finish = jnp.searchsorted(active, base_index + local_count)
    padded_list = jnp.concatenate([active, jnp.zeros((CAP,), jnp.int32)])
    picked = lax.dynamic_slice_in_dim(padded_list, run_begin, CAP)
    occupied = jnp.arange(CAP, dtype=jnp.int32) < finish - run_begin
    local_rows = jnp.where(occupied, picked - base_index, 0)
    filled = occupied.astype(jnp.float32)[None, :]
    own_targets = predicted[:, local_rows] * filled
    partial_value = pull(
        lax.all_gather(own_targets, ("wide", "narrow"), axis=1, tiled=True), sources
    )
    fresh = lax.psum_scatter(partial_value, ("wide", "narrow"), scatter_dimension=1, tiled=True)
    corrected = correct(star_state[:, local_rows], levels[local_rows], fresh)
    return corrected * filled


def solution(mesh):
    placed = (P(None, ("wide", "narrow")), P(("wide", "narrow")), P(("wide", "narrow")), P())
    return jax.shard_map(
        on_device,
        mesh=mesh,
        in_specs=placed,
        out_specs=P(None, ("wide", "narrow")),
        check_vma=False,
    )
```

profile of v0, /device:TPU:1, one launch (start us, length us, event | category | flops | bytes accessed | tf_op | source)
XLA Modules:
  0.0 1220.9 jit_solution(1833528776160846439)
XLA Ops:
  6.5 31.1 %while.43 = (s32[]{:T(128)}, u32[]{:T(128)}, u32[]{:T(128)}, s32[16384]{0:T(1024)}, s32[]{:T(128)}, /*index=5*/s32[]{:T(128)}, u32[]{:T(128)}) while((s32[]{:T(128)}, u32[]{:T(128)}, u32[]{:T(128)}, s32[16384]{0:T(1024)}, s32[]{:T(128)}, /*index=5*/s32[]{:T(128)}, u32[]{:T(128)}) %tuple.92), condition=%wide.region_3.4_spmd, body=%wide.region_2.3_spmd.sunk | while | flops 8 | bytes 160 | solution.py:72
  6.5 1.3 dynamic_slice.25
  8.6 1.4 dynamic_slice.25
  10.7 1.4 dynamic_slice.25
  12.8 1.4 dynamic_slice.25
  14.8 1.4 dynamic_slice.25
  16.9 1.4 dynamic_slice.25
  19.0 1.4 dynamic_slice.25
  21.1 1.4 dynamic_slice.25
  23.1 1.4 dynamic_slice.25
  25.2 1.4 dynamic_slice.25
  27.3 1.4 dynamic_slice.25
  29.3 1.4 dynamic_slice.25
  31.4 1.4 dynamic_slice.25
  33.5 1.4 dynamic_slice.25
  35.6 1.4 dynamic_slice.25
  37.6 29.2 %while.42 = (s32[]{:T(128)}, u32[]{:T(128)}, u32[]{:T(128)}, s32[16384]{0:T(1024)}, s32[]{:T(128)}, /*index=5*/s32[]{:T(128)}, u32[]{:T(128)}) while((s32[]{:T(128)}, u32[]{:T(128)}, u32[]{:T(128)}, s32[16384]{0:T(1024)}, s32[]{:T(128)}, /*index=5*/s32[]{:T(128)}, u32[]{:T(128)}) %tuple.106), condition=%wide.region_1.2_spmd, body=%wide.region_0.1_spmd.sunk | while | flops 8 | bytes 160 | solution.py:73
  49.4 1.3 dynamic_slice.24
  55.2 1.3 dynamic_slice.24
  71.4 198.7 %all-gather.3.cloned.1.call-done = f32[512,96,6]{1,2,0:T(8,128)} async-done(((f32[1,96,6]{1,2,0:T(8,128)}), f32[512,96,6]{1,2,0:T(8,128)}) %all-gather.3.cloned.1.call-update) | async-done | bytes 1179664 | tf_op jit(solution)/shard_map/all_gather | solution.py:81
  270.2 1.9 copy.81
  273.7 107.1 %while.44 = (s32[]{:T(128)}, f32[24,6,2048]{2,1,0:T(8,128)}, f32[1,128]{1,0:T(1,128)S(1)}, f32[3,128]{1,0:T(4,128)S(1)}, f32[24,6,2048]{2,0,1:T(8,128)S(1)}, /*i...) while((s32[]{:T(128)}, f32[24,6,2048]{2,1,0:T(8,128)}, ...), condition=%wide.region_11.12_spmd, body=%wide.region_4.11_spmd.sunk | while | flops 10473479 | bytes 420049 | solution.py:60
  273.8 3.7 fusion.22
  278.3 3.7 fusion.22
  282.7 3.7 fusion.22
  287.2 3.7 fusion.22
  291.6 3.7 fusion.22
  296.1 3.7 fusion.22
  300.6 3.7 fusion.22
  305.0 3.7 fusion.22
  309.5 3.7 fusion.22
  313.9 3.7 fusion.22
  318.4 3.7 fusion.22
  322.9 3.7 fusion.22
  327.3 3.7 fusion.22
  331.8 3.7 fusion.22
  336.2 3.7 fusion.22
  340.7 3.7 fusion.22
  345.2 3.7 fusion.22
  349.6 3.7 fusion.22
  354.1 3.7 fusion.22
  358.5 3.7 fusion.22
  363.0 3.7 fusion.22
  367.5 3.7 fusion.22
  371.9 3.7 fusion.22
  376.4 3.7 fusion.22
  380.8 12.9 %copy.83 = f32[6,49152]{0,1:T(8,128)} copy(f32[6,49152]{1,0:T(8,128)} %bitcast.98) | data formatting | bytes 2359296
  396.4 816.1 %reduce-scatter.4.cloned.1.call-done = f32[96,6]{1,0:T(8,128)} async-done(((f32[49152,6]{1,0:T(8,128)}), f32[96,6]{1,0:T(8,128)}) %reduce-scatter.4.cloned.1.call-update) | async-done | bytes 2320
  (139 shorter events, 45.0 us)
Async XLA Ops:
  6.5 263.6 %all-gather.3.cloned.1.call-start = ((), (), s32[]{:S(2)}) async-start(), calls=%async_computation.1 | async-start | bytes 2101248 | tf_op jit(solution)/shard_map/all_gather | solution.py:81
  70.7 1141.8 %reduce-scatter.4.cloned.1.call-start = ((), (), s32[]{:S(2)}) async-start(), calls=%async_computation.2 | async-start | bytes 25214976
  393.7 0.7 copy-start
  393.7 1.9 copy-start.1
Sparse Core Ops, SparseCore 0:
  70.8 199.2 all-gather.2
  393.9 818.6 reduce-scatter.3
where the time goes:
time: 1230 us; the launch traced here: 1220 us
  waiting for transfers between devices  1010 us (82%)
  other arithmetic  92 us (7%)
  local copies, waits for them, and re-layouts  79 us (6%)
  loops' own time  21.5 us (2%)
  between operations  13.5 us (1%)
    unnamed x3, waiting for transfers between devices  816 us
    all_gather x1, waiting for transfers between devices, on_device(): lax.all_gather(own_targets, ('wide', 'narrow'), axis=1, tiled=True)  199 us
    reduce_sum x24, other arithmetic, pull_block(): jnp.sum(strength * (rel[dim_idx] - radial * sep[dim_idx]), axis=1)  88.3 us
    dynamic_slice x30, local copies, waits for them, and re-layouts, on_device(): finish = jnp.searchsorted(active, base_index + local_count)  39.4 us
  transfers between devices with their start and end apart: 2, of which 2 were waited for; matrix products, arithmetic and copies ran while one was open for 0% of the time, Pallas kernels for 0%

commit v1 on v0

v1 whole, which is shorter than its diff:
```python
import functools

import jax
import jax.numpy as jnp
from jax import lax
from jax.experimental import pallas as pl
from jax.experimental.pallas import tpu as pltpu
from jax.sharding import PartitionSpec as P

MESH = pl.DeviceIdType.MESH
CAP = 96
LANES = 128
GROUP = 64
RING = 8
UNROLL = 16
SOFT = 0.01
BLOCK_COUNTS = (17, 18, 19, 20, 21, 22, 24, 32, 48)


def rows8(row):
    return jnp.broadcast_to(row, (8, LANES))


def lane_gather(tile, idx):
    return jnp.take_along_axis(tile, idx, axis=1, mode="promise_in_bounds")


def step_length(levels):
    return jnp.where(
        levels < 1.5,
        jnp.where(levels < 0.5, 1.0, 0.5),
        jnp.where(levels < 2.5, 0.25, 0.125),
    )


def pull(targets, sources, acc):
    sep = [sources[d] - targets[d] for d in range(3)]
    rel = [sources[3 + d] - targets[3 + d] for d in range(3)]
    dist_sq = (sep[0] * sep[0] + SOFT) + sep[1] * sep[1] + sep[2] * sep[2]
    inverse = lax.rsqrt(dist_sq)
    inverse_sq = inverse * inverse
    strength = (sources[6] * inverse) * inverse_sq
    radial = sep[0] * rel[0] + sep[1] * rel[1] + sep[2] * rel[2]
    turned = (radial * inverse_sq) * strength
    accel = [acc[d] + strength * sep[d] for d in range(3)]
    swing = [acc[3 + d] + strength * rel[d] for d in range(3)]
    drag = [acc[6 + d] + turned * sep[d] for d in range(3)]
    return accel + swing + drag


def kernel(
    blocks, grav, star_ref, mass_ref, level_ref, active_ref, out_ref,
    old, tbuf, zbuf, spread, tgt, offs, accs, fresh, rout, rin,
    tsend, trecv, zsend, zrecv, fsend, frecv, rsend, rrecv,
):
    wide = lax.axis_index("wide")
    narrow = lax.axis_index("narrow")
    plane = wide // 4
    group = (wide % 4) * 2 + narrow // 4
    low = narrow % 4
    member = plane * 4 + low

    def device(plane, group, low):
        return (plane * 4 + group // 2, (group % 2) * 4 + low)

    def mate(i):
        other = (member + i) % GROUP
        return other, device(other // 4, group, other % 4)

    def along(shift):
        return device(plane, (group + shift + RING) % RING, low)

    barrier = pltpu.get_barrier_semaphore()

    def greet(i, carry):
        pl.semaphore_signal(barrier, inc=1, device_id=mate(i)[1], device_id_type=MESH)
        return carry

    for shift in (-2, 2, -1, 1):
        pl.semaphore_signal(barrier, inc=1, device_id=along(shift), device_id_type=MESH)
    lax.fori_loop(1, GROUP, greet, 0)

    lane = lax.broadcasted_iota(jnp.int32, (8, LANES), 1)
    sub = lax.broadcasted_iota(jnp.int32, (8, LANES), 0)
    star = [star_ref[d : d + 1, :] for d in range(12)]
    step = step_length(level_ref[...].astype(jnp.float32))
    pred = []
    for d in range(3):
        x, v, a, j = star[d], star[3 + d], star[6 + d], star[9 + d]
        pred.append(x + step * (v + step * (a * 0.5 + step * j * (1.0 / 6.0))))
    for d in range(3):
        v, a, j = star[3 + d], star[6 + d], star[9 + d]
        pred.append(v + step * (a + step * j * 0.5))
    for d in range(6):
        zbuf[0, d : d + 1, :] = pred[d]
    zbuf[0, 6:7, :] = mass_ref[...] * grav
    zbuf[0, 7:8, :] = jnp.zeros((1, LANES), jnp.float32)

    base = (wide * 8 + narrow) * LANES
    below = jnp.zeros((8, LANES), jnp.int32)
    through = jnp.zeros((8, LANES), jnp.int32)
    for v in range(16):
        entry = active_ref[8 * v : 8 * v + 8, :]
        below = below + jnp.where(entry < base, 1, 0)
        through = through + jnp.where(entry < base + LANES, 1, 0)

    def total(x):
        s = jnp.sum(x.astype(jnp.float32), axis=0, keepdims=True)
        s = jnp.sum(s, axis=1, keepdims=True)
        return jnp.broadcast_to(s, (8, LANES)).astype(jnp.int32)

    begin = total(below)
    count = total(through) - begin
    row_of = lax.shift_right_logical(begin + ((lane - begin) & (LANES - 1)), 7)
    found = jnp.zeros((8, LANES), jnp.int32)
    for v in range(16):
        entry = active_ref[8 * v : 8 * v + 8, :]
        found = found + jnp.where(row_of == sub + 8 * v, entry, 0)
    found = jnp.sum(found.astype(jnp.float32), axis=0, keepdims=True).astype(jnp.int32)
    picked = lane_gather(rows8(found), (lane + begin) & (LANES - 1)) - base
    picked = jnp.where(lane < count, picked, 0) & (LANES - 1)

    chosen = lane_gather(zbuf[0], picked)
    chosen = jnp.where(sub == 6, count.astype(jnp.float32), chosen)
    tbuf[member] = chosen

    pl.semaphore_wait(barrier, GROUP - 1 + 4)

    def send_target(i, carry):
        pltpu.make_async_remote_copy(
            src_ref=tbuf.at[member], dst_ref=tbuf.at[member],
            send_sem=tsend, recv_sem=trecv, device_id=mate(i)[1], device_id_type=MESH,
        ).start()
        return carry

    for slot in (2, 6, 1, 7):
        pltpu.make_async_remote_copy(
            src_ref=zbuf.at[0], dst_ref=zbuf.at[slot],
            send_sem=zsend, recv_sem=zrecv, device_id=along(-slot), device_id_type=MESH,
        ).start()
    lax.fori_loop(1, GROUP, send_target, 0)

    old[0:8, :] = lane_gather(star_ref[0:8, :], picked)
    old[8:12, :] = star_ref[8:12, :]
    old[12:13, :] = step
    old[13:16, :] = jnp.zeros((3, LANES), jnp.float32)
    old[8:16, :] = lane_gather(old[8:16, :], picked)

    def spread_tile(slot, place):
        turned = zbuf[slot].T
        for d in range(7):
            spread[d, place * LANES : (place + 1) * LANES, :] = jnp.broadcast_to(
                turned[:, d : d + 1], (LANES, LANES)
            )

    spread_tile(0, 0)

    four = zbuf.at[pl.ds(0, 4)]
    three = zbuf.at[pl.ds(0, 3)]
    pltpu.make_async_copy(four, four, zrecv).wait()
    far_a = pltpu.make_async_remote_copy(
        src_ref=zbuf.at[pl.ds(1, 2)], dst_ref=zbuf.at[pl.ds(3, 2)],
        send_sem=fsend, recv_sem=frecv, device_id=along(-2), device_id_type=MESH,
    )
    far_b = pltpu.make_async_remote_copy(
        src_ref=zbuf.at[7], dst_ref=zbuf.at[5],
        send_sem=fsend, recv_sem=frecv, device_id=along(2), device_id_type=MESH,
    )
    far_a.start()
    far_b.start()
    for place, slot in ((1, 1), (2, 2), (3, 6), (4, 7)):
        spread_tile(slot, place)

    others = tbuf.at[pl.ds(0, GROUP - 1)]
    pltpu.make_async_copy(others, others, trecv).wait()

    def lay(o, carry):
        off = carry[0]
        tile = tbuf[o]
        offs[o] = off
        rolled = lane_gather(tile, (lane - off) & (LANES - 1))
        laid = [
            jnp.where(lane + LANES * b >= off, rolled, carry[1 + b]) for b in range(blocks)
        ]
        return (off + rows8(tile[6:7, :]).astype(jnp.int32), *laid)

    laid = lax.fori_loop(
        0, GROUP, lay,
        (jnp.zeros((8, LANES), jnp.int32),) + (jnp.zeros((8, LANES), jnp.float32),) * blocks,
    )
    for b in range(blocks):
        tgt[b] = laid[1 + b]

    def pairs(b, acc, first, chunks):
        targets = [rows8(tgt[b, d : d + 1, :]) for d in range(6)]

        def chunk(k, acc):
            acc = list(acc)
            for u in range(UNROLL):
                place = pl.ds(pl.multiple_of((first + k) * (8 * UNROLL) + 8 * u, 8), 8)
                acc = pull(targets, [spread[d, place, :] for d in range(7)], acc)
            return tuple(acc)

        return lax.fori_loop(0, chunks, chunk, acc)

    def near(b, carry):
        acc = pairs(b, (jnp.zeros((8, LANES), jnp.float32),) * 9, 0, 5)
        for d in range(9):
            accs[b, d] = acc[d]
        return carry

    lax.fori_loop(0, blocks, near, 0)

    pltpu.make_async_copy(three, three, frecv).wait()
    for place, slot in ((5, 3), (6, 4), (7, 5)):
        spread_tile(slot, place)

    def far(b, carry):
        acc = pairs(b, tuple(accs[b, d] for d in range(9)), 5, 3)
        for d in range(3):
            fresh[b, d : d + 1, :] = jnp.sum(acc[d], axis=0, keepdims=True)
            fresh[b, 3 + d : 4 + d, :] = jnp.sum(acc[3 + d] - 3.0 * acc[6 + d], axis=0, keepdims=True)
        fresh[b, 6:8, :] = jnp.zeros((2, LANES), jnp.float32)
        return carry

    lax.fori_loop(0, blocks, far, 0)

    def cut(o):
        off = offs[o]
        block_of = lax.shift_right_logical(off + ((lane - off) & (LANES - 1)), 7)
        mine = fresh[0]
        for b in range(1, blocks):
            mine = jnp.where(block_of == b, fresh[b], mine)
        return lane_gather(mine, (lane + off) & (LANES - 1))

    def give(i, carry):
        o, where = mate(i)
        rout[o] = cut(o)
        pltpu.make_async_remote_copy(
            src_ref=rout.at[o], dst_ref=rin.at[member],
            send_sem=rsend, recv_sem=rrecv, device_id=where, device_id_type=MESH,
        ).start()
        return carry

    lax.fori_loop(1, GROUP, give, 0)
    rin[member] = cut(member)

    back = rin.at[pl.ds(0, GROUP - 1)]
    pltpu.make_async_copy(back, back, rrecv).wait()
    sums = [rin[m] for m in range(8)]
    for m in range(8, GROUP):
        sums[m % 8] = sums[m % 8] + rin[m]
    while len(sums) > 1:
        sums = [sums[i] + sums[i + 1] for i in range(0, len(sums), 2)]
    new = sums[0]

    filled = lane[0:1, :] < count[0:1, :]
    step = old[12:13, :]
    half = step * 0.5
    twelfth = step * step * (1.0 / 12.0)
    for d in range(3):
        x0, v0 = old[d : d + 1, :], old[3 + d : 4 + d, :]
        a0, j0 = old[6 + d : 7 + d, :], old[9 + d : 10 + d, :]
        a1, j1 = new[d : d + 1, :], new[3 + d : 4 + d, :]
        v1 = v0 + half * (a0 + a1) + twelfth * (j0 - j1)
        x1 = x0 + half * (v0 + v1) + twelfth * (a0 - a1)
        for r, value in ((d, x1), (3 + d, v1), (6 + d, a1), (9 + d, j1)):
            out_ref[r : r + 1, :] = jnp.where(filled, value, 0.0)[:, :CAP]

    pltpu.make_async_copy(others, others, tsend).wait()
    pltpu.make_async_copy(four, four, zsend).wait()
    pltpu.make_async_copy(three, three, fsend).wait()
    pltpu.make_async_copy(back, back, rsend).wait()


def on_device(star_state, masses, levels, active):
    local_count = star_state.shape[1]
    owners = lax.axis_size(("wide", "narrow"))
    grav = 1.0 / (local_count * owners)
    tile = (8, LANES)
    dma = pltpu.SemaphoreType.DMA

    def branch(which, blocks):
        return pl.pallas_call(
            functools.partial(kernel, blocks, grav),
            out_shape=jax.ShapeDtypeStruct((12, CAP), jnp.float32),
            in_specs=[pl.BlockSpec(memory_space=pltpu.VMEM)] * 4,
            out_specs=pl.BlockSpec(memory_space=pltpu.VMEM),
            scratch_shapes=[
                pltpu.VMEM((16, LANES), jnp.float32),
                pltpu.VMEM((GROUP, *tile), jnp.float32),
                pltpu.VMEM((RING, *tile), jnp.float32),
                pltpu.VMEM((7, RING * LANES, LANES), jnp.float32),
                pltpu.VMEM((blocks, *tile), jnp.float32),
                pltpu.VMEM((GROUP, *tile), jnp.int32),
                pltpu.VMEM((blocks, 9, *tile), jnp.float32),
                pltpu.VMEM((blocks, *tile), jnp.float32),
                pltpu.VMEM((GROUP, *tile), jnp.float32),
                pltpu.VMEM((GROUP, *tile), jnp.float32),
            ]
            + [dma(())] * 8,
            compiler_params=pltpu.CompilerParams(
                collective_id=which, has_side_effects=True, vmem_limit_bytes=32 << 20
            ),
            name=f"step_{blocks}",
        )

    group_of = lax.shift_right_logical(active, 9) & 7
    counts = jnp.sum(
        (group_of[None, :] == jnp.arange(RING, dtype=jnp.int32)[:, None]).astype(jnp.int32), axis=1
    )
    most = jnp.max(counts)
    limits = jnp.array([b * LANES for b in BLOCK_COUNTS[:-1]], jnp.int32)
    which = jnp.sum((most > limits).astype(jnp.int32))
    return lax.switch(
        which,
        [branch(i, b) for i, b in enumerate(BLOCK_COUNTS)],
        star_state, masses.reshape(1, LANES), levels.reshape(1, LANES),
        active.reshape(LANES, LANES),
    )


def solution(mesh):
    placed = (P(None, ("wide", "narrow")), P(("wide", "narrow")), P(("wide", "narrow")), P())
    return jax.shard_map(
        on_device,
        mesh=mesh,
        in_specs=placed,
        out_specs=P(None, ("wide", "narrow")),
        check_vma=False,
    )
```

time: 1230 us -> 54.6 us (0.04)
  waiting for transfers between devices: 1010 us -> 0 us
  other arithmetic: 92 us -> 3.1 us
  local copies, waits for them, and re-layouts: 79 us -> 0.64 us
  Pallas kernels: 0 us -> 49.6 us
  loops' own time: 21.5 us -> 0.27 us
  between operations: 13.5 us -> 0.78 us
    unnamed x3 -> x0, waiting for transfers between devices: 816 us -> none
    all_gather x1 -> x0, waiting for transfers between devices: 199 us -> none  [on_device(): lax.all_gather(own_targets, ('wide', 'narrow'), axis=1, tiled=True)]
    reduce_sum x24 -> x2, other arithmetic: 88.3 us -> 1.6 us  [the longest x1 1.35 us: on_device(): which = jnp.sum((most > limits).astype(jnp.int32))]
    pallas_call x0 -> x1, Pallas kernels: none -> 49.6 us  [on_device(): lax.switch(which, [branch(i, b) for i, b in enumerate(BLOCK_COUNTS)], sta...]
    dynamic_slice x30 -> x0, local copies, waits for them, and re-layouts: 39.4 us -> none  [on_device(): finish = jnp.searchsorted(active, base_index + local_count)]
    another operation x3 -> x1, loops' own time: 21.5 us -> 0.27 us  [on_device(): lax.switch(which, [branch(i, b) for i, b in enumerate(BLOCK_COUNTS)], sta...]
    unnamed x10 -> x11, local copies, waits for them, and re-layouts: 16.9 us -> 0.64 us
    dynamic_update_slice x24 -> x0, local copies, waits for them, and re-layouts: 15.1 us -> none  [pull(): lax.map(lambda tile_block: pull_block(tile_block, sources), grouped)]
  transfers between devices with their start and end apart: 2 -> 0, of which waited for: 2 -> 0; matrix products, arithmetic and copies ran while one was open for 0% -> 0% of each run, Pallas kernels for 0% -> 0%
where the time goes in v1:
time: 54.6 us; the launch traced here: 54.4 us
  Pallas kernels  49.6 us (91%)
  other arithmetic  3.1 us (6%)
  between operations  0.78 us (1%)
  local copies, waits for them, and re-layouts  0.64 us (1%)
    pallas_call x1, Pallas kernels, on_device(): lax.switch(which, [branch(i, b) for i, b in enumerate(BLOCK_COUNTS)], sta...  49.6 us
    reduce_sum x1, other arithmetic, on_device(): which = jnp.sum((most > limits).astype(jnp.int32))  1.35 us

profile of v1, /device:TPU:1, one launch (start us, length us, event | category | flops | bytes accessed | tf_op | source)
XLA Modules:
  0.0 54.4 jit_solution(14425475065639325855)
XLA Ops:
  0.0 0.0 copy-start.1
  0.0 0.9 %shift-right-logical_and_fusion = s32[16384]{0:T(1024)S(1)} fusion(s32[16384]{0:T(1024)} %param.17), kind=kLoop, calls=%fused_computation.2 | loop fusion | flops 32768 | bytes 131072 | tf_op jit(solution)/shard_map/and | solution.py:308
  0.9 0.0 copy-start
  0.9 0.2 convert_reduce_fusion
  1.1 0.0 copy-start.4
  1.1 0.6 %reduce_max.9 = s32[]{:T(128)} reduce(s32[8]{0:T(128)S(1)} %convert_reduce_fusion, s32[]{:T(128)} %constant.4.clone.1), dimensions={0}, to_apply=%region_1.0 | reduce | flops 7 | bytes 40 | tf_op jit(solution)/shard_map/reduce_max | solution.py:312
  1.8 0.0 copy-done.4
  1.8 1.4 %fusion = s32[]{:T(128)} fusion(s32[8]{0:T(128)S(1)} %copy-done.4, s32[]{:T(128)} %reduce_max.9), kind=kLoop, calls=%fused_computation.4 | loop fusion | flops 23 | bytes 40 | tf_op jit(solution)/shard_map/reduce_sum | solution.py:314
  3.1 0.0 copy-start.2
  3.1 0.0 copy-start.3
  3.9 0.0 copy-done.1
  3.9 0.0 copy-done
  3.9 0.0 copy-done.2
  3.9 0.0 copy-done.3
  3.9 49.9 %conditional.1 = (f32[12,96]{1,0:T(8,128)S(1)}) conditional(s32[]{:T(128)} %clamp.3, (f32[12,128]{1,0:T(8,128)S(1)}, f32[128]{0:T(128)S(1)}, s32[128]{0:T(128)S(1)}, s32[16384]{0:T(1024)S(1)}) %tuple.78, (f32[12,128]{1,0:T(8,128)S(1)}, f32[128]{0:T(128)S(1)}, s32[128]{0:T(128)S(1)}, s32[16384]{0:T(1024)S(1)}) %tuple.79, ...), branch_computations={%region_3.0_spmd, %region_4.0_spmd, %region_5.0_spmd, %region_6.0_... | conditional | bytes 8 | solution.py:315
  3.9 49.6 %step_18.1 = f32[12,96]{1,0:T(8,128)S(1)} custom-call(f32[12,128]{1,0:T(8,128)S(1)} %get-tuple-element.161.star_ref, f32[1,128]{1,0:T(1,128)S(1)} %bitcast.37, s32[1,128]{1,0:T(1,128)S(1)} %bitcast.46, s32[128,128]{1,0:T(8,128)S(1)} %bitcast.28), custom_call_target="tpu_custom_call" | custom-call | tf_op jit(solution)/shard_map/cond/branch_1_fun/step_18/pallas_call | solution.py:315
  53.8 0.6 %copy.52 = f32[12,96]{1,0:T(8,128)} copy(f32[12,96]{1,0:T(8,128)S(1)} %get-tuple-element.123) | data formatting | bytes 9216
Async XLA Ops:
  0.0 3.9 %copy-start.1 = (f32[12,128]{1,0:T(8,128)S(1)}, f32[12,128]{1,0:T(8,128)}, u32[]{:S(2)}) copy-start(f32[12,128]{1,0:T(8,128)} %param.14) | copy-start | bytes 18436
  0.9 3.0 %copy-start = (s32[16384]{0:T(1024)S(1)}, s32[16384]{0:T(1024)}, u32[]{:S(2)}) copy-start(s32[16384]{0:T(1024)} %param.17) | copy-start | bytes 196612
  1.1 0.7 %copy-start.4 = (s32[8]{0:T(128)S(1)}, s32[8]{0:T(128)}, u32[]{:S(2)}) copy-start(s32[8]{0:T(128)} %constant.12.clone) | copy-start | bytes 100
  3.1 0.8 %copy-start.2 = (f32[128]{0:T(128)S(1)}, f32[128]{0:T(128)}, u32[]{:S(2)}) copy-start(f32[128]{0:T(128)} %param.15) | copy-start | bytes 1540
  3.1 0.8 %copy-start.3 = (s32[128]{0:T(128)S(1)}, s32[128]{0:T(128)}, u32[]{:S(2)}) copy-start(s32[128]{0:T(128)} %param.16) | copy-start | bytes 1540

commit v2 on v1

--- a/solution.py
+++ b/solution.py
@@ -10,11 +10,17 @@
 MESH = pl.DeviceIdType.MESH
 CAP = 96
 LANES = 128
-GROUP = 64
-RING = 8
-UNROLL = 16
+GROUP = 32
+RING = 16
+REACH = 4
+UNROLL = 32
+NEAR = (-4, 4, -3, 3, -2, 2, -1, 1)
+EARLY = (0, 1, 15, 2, 14, 3, 13, 4)
+HALF = RING * LANES // (16 * UNROLL)
+LATE = (12, 5, 6, 7, 8, 9, 10, 11)
+ROWS = 6
 SOFT = 0.01
-BLOCK_COUNTS = (17, 18, 19, 20, 21, 22, 24, 32, 48)
+BLOCK_COUNTS = (10, 11, 12, 13, 14, 16, 20, 24)
 
 
 def rows8(row):
@@ -49,26 +55,26 @@
 
 
 def kernel(
-    blocks, grav, star_ref, mass_ref, level_ref, active_ref, out_ref,
+    blocks, state_hbm, active_hbm, out_ref, state, active_ref,
     old, tbuf, zbuf, spread, tgt, offs, accs, fresh, rout, rin,
-    tsend, trecv, zsend, zrecv, fsend, frecv, rsend, rrecv,
+    load, tsend, trecv, zsend, zrecv, fsend, frecv, rsend, rrecv,
 ):
     wide = lax.axis_index("wide")
     narrow = lax.axis_index("narrow")
     plane = wide // 4
-    group = (wide % 4) * 2 + narrow // 4
-    low = narrow % 4
-    member = plane * 4 + low
-
-    def device(plane, group, low):
-        return (plane * 4 + group // 2, (group % 2) * 4 + low)
+    level = (wide % 4) * 4 + narrow // 2
+    core = narrow % 2
+    member = plane * 2 + core
+
+    def device(plane, level, core):
+        return (plane * 4 + level // 4, (level % 4) * 2 + core)
 
     def mate(i):
         other = (member + i) % GROUP
-        return other, device(other // 4, group, other % 4)
+        return other, device(other // 2, level, other % 2)
 
     def along(shift):
-        return device(plane, (group + shift + RING) % RING, low)
+        return device(plane, (level + shift + RING) % RING, core)
 
     barrier = pltpu.get_barrier_semaphore()
 
@@ -76,14 +82,23 @@
         pl.semaphore_signal(barrier, inc=1, device_id=mate(i)[1], device_id_type=MESH)
         return carry
 
-    for shift in (-2, 2, -1, 1):
+    for shift in NEAR:
         pl.semaphore_signal(barrier, inc=1, device_id=along(shift), device_id_type=MESH)
     lax.fori_loop(1, GROUP, greet, 0)
 
+    loads = [
+        pltpu.make_async_copy(state_hbm, state, load.at[0]),
+        pltpu.make_async_copy(active_hbm, active_ref, load.at[1]),
+    ]
+    for copy in loads:
+        copy.start()
+    for copy in loads:
+        copy.wait()
+
     lane = lax.broadcasted_iota(jnp.int32, (8, LANES), 1)
     sub = lax.broadcasted_iota(jnp.int32, (8, LANES), 0)
-    star = [star_ref[d : d + 1, :] for d in range(12)]
-    step = step_length(level_ref[...].astype(jnp.float32))
+    star = [state[d : d + 1, :] for d in range(12)]
+    step = state[12:13, :]
     pred = []
     for d in range(3):
         x, v, a, j = star[d], star[3 + d], star[6 + d], star[9 + d]
@@ -93,7 +108,7 @@
         pred.append(v + step * (a + step * j * 0.5))
     for d in range(6):
         zbuf[0, d : d + 1, :] = pred[d]
-    zbuf[0, 6:7, :] = mass_ref[...] * grav
+    zbuf[0, 6:7, :] = state[13:14, :]
     zbuf[0, 7:8, :] = jnp.zeros((1, LANES), jnp.float32)
 
     base = (wide * 8 + narrow) * LANES
@@ -121,30 +136,27 @@
     picked = jnp.where(lane < count, picked, 0) & (LANES - 1)
 
     chosen = lane_gather(zbuf[0], picked)
-    chosen = jnp.where(sub == 6, count.astype(jnp.float32), chosen)
+    chosen = jnp.where(lane == LANES - 1, count.astype(jnp.float32), chosen)
     tbuf[member] = chosen
 
-    pl.semaphore_wait(barrier, GROUP - 1 + 4)
+    pl.semaphore_wait(barrier, GROUP - 1 + len(NEAR))
 
     def send_target(i, carry):
         pltpu.make_async_remote_copy(
-            src_ref=tbuf.at[member], dst_ref=tbuf.at[member],
+            src_ref=tbuf.at[member, pl.ds(0, ROWS)], dst_ref=tbuf.at[member, pl.ds(0, ROWS)],
             send_sem=tsend, recv_sem=trecv, device_id=mate(i)[1], device_id_type=MESH,
         ).start()
         return carry
 
-    for slot in (2, 6, 1, 7):
+    for shift in NEAR:
         pltpu.make_async_remote_copy(
-            src_ref=zbuf.at[0], dst_ref=zbuf.at[slot],
-            send_sem=zsend, recv_sem=zrecv, device_id=along(-slot), device_id_type=MESH,
+            src_ref=zbuf.at[0], dst_ref=zbuf.at[(RING - shift) % RING],
+            send_sem=zsend, recv_sem=zrecv, device_id=along(shift), device_id_type=MESH,
         ).start()
     lax.fori_loop(1, GROUP, send_target, 0)
 
-    old[0:8, :] = lane_gather(star_ref[0:8, :], picked)
-    old[8:12, :] = star_ref[8:12, :]
-    old[12:13, :] = step
-    old[13:16, :] = jnp.zeros((3, LANES), jnp.float32)
-    old[8:16, :] = lane_gather(old[8:16, :], picked)
+    old[0:8, :] = lane_gather(state[0:8, :], picked)
+    old[8:16, :] = lane_gather(state[8:16, :], picked)
 
     def spread_tile(slot, place):
         turned = zbuf[slot].T
@@ -155,37 +167,39 @@
 
     spread_tile(0, 0)
 
-    four = zbuf.at[pl.ds(0, 4)]
-    three = zbuf.at[pl.ds(0, 3)]
-    pltpu.make_async_copy(four, four, zrecv).wait()
-    far_a = pltpu.make_async_remote_copy(
-        src_ref=zbuf.at[pl.ds(1, 2)], dst_ref=zbuf.at[pl.ds(3, 2)],
-        send_sem=fsend, recv_sem=frecv, device_id=along(-2), device_id_type=MESH,
-    )
-    far_b = pltpu.make_async_remote_copy(
-        src_ref=zbuf.at[7], dst_ref=zbuf.at[5],
-        send_sem=fsend, recv_sem=frecv, device_id=along(2), device_id_type=MESH,
-    )
-    far_a.start()
-    far_b.start()
-    for place, slot in ((1, 1), (2, 2), (3, 6), (4, 7)):
-        spread_tile(slot, place)
-
-    others = tbuf.at[pl.ds(0, GROUP - 1)]
+    direct = zbuf.at[pl.ds(0, len(NEAR))]
+    passed = zbuf.at[pl.ds(0, RING - 1 - len(NEAR))]
+    pltpu.make_async_copy(direct, direct, zrecv).wait()
+    pltpu.make_async_remote_copy(
+        src_ref=zbuf.at[pl.ds(1, REACH)], dst_ref=zbuf.at[pl.ds(1 + REACH, REACH)],
+        send_sem=fsend, recv_sem=frecv, device_id=along(-REACH), device_id_type=MESH,
+    ).start()
+    pltpu.make_async_remote_copy(
+        src_ref=zbuf.at[pl.ds(RING - REACH + 1, REACH - 1)],
+        dst_ref=zbuf.at[pl.ds(RING - 2 * REACH + 1, REACH - 1)],
+        send_sem=fsend, recv_sem=frecv, device_id=along(REACH), device_id_type=MESH,
+    ).start()
+    for place, slot in enumerate(EARLY[1:]):
+        spread_tile(slot, 1 + place)
+
+    others = tbuf.at[pl.ds(0, GROUP - 1), pl.ds(0, ROWS)]
     pltpu.make_async_copy(others, others, trecv).wait()
 
-    def lay(o, carry):
-        off = carry[0]
-        tile = tbuf[o]
-        offs[o] = off
-        rolled = lane_gather(tile, (lane - off) & (LANES - 1))
-        laid = [
-            jnp.where(lane + LANES * b >= off, rolled, carry[1 + b]) for b in range(blocks)
-        ]
-        return (off + rows8(tile[6:7, :]).astype(jnp.int32), *laid)
+    def lay(k, carry):
+        off, laid = carry[0], carry[1:]
+        for u in range(8):
+            o = k * 8 + u
+            tile = tbuf[o]
+            offs[o] = off
+            rolled = lane_gather(tile, (lane - off) & (LANES - 1))
+            laid = [jnp.where(lane + LANES * b >= off, rolled, laid[b]) for b in range(blocks)]
+            off = off + rows8(
+                jnp.broadcast_to(tile[0:1, LANES - 1 : LANES], (1, LANES))
+            ).astype(jnp.int32)
+        return (off, *laid)
 
     laid = lax.fori_loop(
-        0, GROUP, lay,
+        0, GROUP // 8, lay,
         (jnp.zeros((8, LANES), jnp.int32),) + (jnp.zeros((8, LANES), jnp.float32),) * blocks,
     )
     for b in range(blocks):
@@ -204,19 +218,19 @@
         return lax.fori_loop(0, chunks, chunk, acc)
 
     def near(b, carry):
-        acc = pairs(b, (jnp.zeros((8, LANES), jnp.float32),) * 9, 0, 5)
+        acc = pairs(b, (jnp.zeros((8, LANES), jnp.float32),) * 9, 0, HALF)
         for d in range(9):
             accs[b, d] = acc[d]
         return carry
 
     lax.fori_loop(0, blocks, near, 0)
 
-    pltpu.make_async_copy(three, three, frecv).wait()
-    for place, slot in ((5, 3), (6, 4), (7, 5)):
-        spread_tile(slot, place)
+    pltpu.make_async_copy(passed, passed, frecv).wait()
+    for place, slot in enumerate(LATE):
+        spread_tile(slot, len(EARLY) + place)
 
     def far(b, carry):
-        acc = pairs(b, tuple(accs[b, d] for d in range(9)), 5, 3)
+        acc = pairs(b, tuple(accs[b, d] for d in range(9)), HALF, HALF)
         for d in range(3):
             fresh[b, d : d + 1, :] = jnp.sum(acc[d], axis=0, keepdims=True)
             fresh[b, 3 + d : 4 + d, :] = jnp.sum(acc[3 + d] - 3.0 * acc[6 + d], axis=0, keepdims=True)
@@ -233,19 +247,24 @@
             mine = jnp.where(block_of == b, fresh[b], mine)
         return lane_gather(mine, (lane + off) & (LANES - 1))
 
-    def give(i, carry):
-        o, where = mate(i)
-        rout[o] = cut(o)
-        pltpu.make_async_remote_copy(
-            src_ref=rout.at[o], dst_ref=rin.at[member],
-            send_sem=rsend, recv_sem=rrecv, device_id=where, device_id_type=MESH,
-        ).start()
-        return carry
-
-    lax.fori_loop(1, GROUP, give, 0)
+    def give(first, count):
+        cuts = [(mate(first + u), cut(mate(first + u)[0])) for u in range(count)]
+        for (o, where), mine in cuts:
+            rout[o] = mine
+            pltpu.make_async_remote_copy(
+                src_ref=rout.at[o, pl.ds(0, ROWS)], dst_ref=rin.at[member, pl.ds(0, ROWS)],
+                send_sem=rsend, recv_sem=rrecv, device_id=where, device_id_type=MESH,
+            ).start()
+
+    def give8(k, carry):
+        give(1 + 8 * k, 8)
+        return carry
+
+    lax.fori_loop(0, GROUP // 8 - 1, give8, 0)
+    give(GROUP - 7, 7)
     rin[member] = cut(member)
 
-    back = rin.at[pl.ds(0, GROUP - 1)]
+    back = rin.at[pl.ds(0, GROUP - 1), pl.ds(0, ROWS)]
     pltpu.make_async_copy(back, back, rrecv).wait()
     sums = [rin[m] for m in range(8)]
     for m in range(8, GROUP):
@@ -268,9 +287,24 @@
             out_ref[r : r + 1, :] = jnp.where(filled, value, 0.0)[:, :CAP]
 
     pltpu.make_async_copy(others, others, tsend).wait()
-    pltpu.make_async_copy(four, four, zsend).wait()
-    pltpu.make_async_copy(three, three, fsend).wait()
+    pltpu.make_async_copy(direct, direct, zsend).wait()
+    pltpu.make_async_copy(passed, passed, fsend).wait()
     pltpu.make_async_copy(back, back, rsend).wait()
+
+
+def prepare(grav, active_ref, star_ref, mass_ref, level_ref, which_ref, state_ref):
+    state_ref[0:12, :] = star_ref[...]
+    state_ref[12:13, :] = step_length(level_ref[...].astype(jnp.float32))
+    state_ref[13:14, :] = mass_ref[...] * grav
+    state_ref[14:16, :] = jnp.zeros((2, LANES), jnp.float32)
+
+    counts = [jnp.zeros((8, LANES), jnp.int32) for _ in range(RING)]
+    for v in range(16):
+        plane = lax.shift_right_logical(active_ref[8 * v : 8 * v + 8, :], 8) & (RING - 1)
+        counts = [c + jnp.where(plane == g, 1, 0) for g, c in enumerate(counts)]
+    rows = [jnp.sum(c.astype(jnp.float32), axis=0, keepdims=True) for c in counts]
+    most = jnp.max(jnp.sum(jnp.concatenate(rows, axis=0), axis=1, keepdims=True))
+    which_ref[0] = sum(jnp.where(most > b * LANES, 1, 0) for b in BLOCK_COUNTS[:-1])
 
 
 def on_device(star_state, masses, levels, active):
@@ -282,11 +316,13 @@
 
     def branch(which, blocks):
         return pl.pallas_call(
-            functools.partial(kernel, blocks, grav),
+            functools.partial(kernel, blocks),
             out_shape=jax.ShapeDtypeStruct((12, CAP), jnp.float32),
-            in_specs=[pl.BlockSpec(memory_space=pltpu.VMEM)] * 4,
+            in_specs=[pl.BlockSpec(memory_space=pl.ANY)] * 2,
             out_specs=pl.BlockSpec(memory_space=pltpu.VMEM),
             scratch_shapes=[
+                pltpu.VMEM((16, LANES), jnp.float32),
+                pltpu.VMEM((LANES, LANES), jnp.int32),
                 pltpu.VMEM((16, LANES), jnp.float32),
                 pltpu.VMEM((GROUP, *tile), jnp.float32),
                 pltpu.VMEM((RING, *tile), jnp.float32),
@@ -297,26 +333,29 @@
                 pltpu.VMEM((blocks, *tile), jnp.float32),
                 pltpu.VMEM((GROUP, *tile), jnp.float32),
                 pltpu.VMEM((GROUP, *tile), jnp.float32),
+                dma((2,)),
             ]
             + [dma(())] * 8,
             compiler_params=pltpu.CompilerParams(
-                collective_id=which, has_side_effects=True, vmem_limit_bytes=32 << 20
+                collective_id=which, has_side_effects=True, vmem_limit_bytes=40 << 20
             ),
             name=f"step_{blocks}",
         )
 
-    group_of = lax.shift_right_logical(active, 9) & 7
-    counts = jnp.sum(
-        (group_of[None, :] == jnp.arange(RING, dtype=jnp.int32)[:, None]).astype(jnp.int32), axis=1
-    )
-    most = jnp.max(counts)
-    limits = jnp.array([b * LANES for b in BLOCK_COUNTS[:-1]], jnp.int32)
-    which = jnp.sum((most > limits).astype(jnp.int32))
+    listed = active.reshape(LANES, LANES)
+    which, state = pl.pallas_call(
+        functools.partial(prepare, grav),
+        out_shape=(
+            jax.ShapeDtypeStruct((1,), jnp.int32), jax.ShapeDtypeStruct((16, LANES), jnp.float32),
+        ),
+        in_specs=[pl.BlockSpec(memory_space=pltpu.VMEM)] * 4,
+        out_specs=(
+            pl.BlockSpec(memory_space=pltpu.SMEM), pl.BlockSpec(memory_space=pltpu.VMEM),
+        ),
+        name="prepare",
+    )(listed, star_state, masses.reshape(1, LANES), levels.reshape(1, LANES))
     return lax.switch(
-        which,
-        [branch(i, b) for i, b in enumerate(BLOCK_COUNTS)],
-        star_state, masses.reshape(1, LANES), levels.reshape(1, LANES),
-        active.reshape(LANES, LANES),
+        which[0], [branch(i, b) for i, b in enumerate(BLOCK_COUNTS)], state, listed
     )
 
 

time: 54.6 us -> 48.4 us (0.89)
  Pallas kernels: 49.6 us -> 46.4 us
  other arithmetic: 3.1 us -> 0 us
    pallas_call x1 -> x2, Pallas kernels: 49.6 us -> 46.4 us  [the longest x1 44.7 us: on_device(): lax.switch(which[0], [branch(i, b) for i, b in enumerate(BLOCK_COUNTS)],...]
    reduce_sum x2 -> x0, other arithmetic: 1.6 us -> none  [the longest x1 1.35 us: on_device(): which = jnp.sum((most > limits).astype(jnp.int32))]
    and x1 -> x0, other arithmetic: 0.86 us -> none  [on_device(): group_of = lax.shift_right_logical(active, 9) & 7]
    reduce_max x1 -> x0, other arithmetic: 0.63 us -> none  [on_device(): most = jnp.max(counts)]
where the time goes in v2:
time: 48.4 us; the launch traced here: 48.3 us
  Pallas kernels  46.4 us (96%)
  between operations  0.67 us (1%)
  local copies, waits for them, and re-layouts  0.6 us (1%)
  loops' own time  0.57 us (1%)
    pallas_call x1, Pallas kernels, on_device(): lax.switch(which[0], [branch(i, b) for i, b in enumerate(BLOCK_COUNTS)],...  44.7 us
    pallas_call x1, Pallas kernels, on_device(): pl.pallas_call(functools.partial(prepare, grav), out_shape=(jax.ShapeDtyp...  1.68 us

profile of v2, /device:TPU:1, one launch (start us, length us, event | category | flops | bytes accessed | tf_op | source)
XLA Modules:
  0.0 48.3 jit_solution(4762784582256961349)
XLA Ops:
  0.0 0.0 copy-start
  0.0 1.7 %prepare.1 = (s32[1]{0:T(128)}, f32[16,128]{1,0:T(8,128)S(1)}) custom-call(s32[128,128]{1,0:T(8,128)} %bitcast.4, f32[12,128]{1,0:T(8,128)} %star_ref.1, f32[1,128]{1,0:T(1,128)} %bitcast.13, s32[1,128]{1,0:T(1,128)} %bitcast.14), custom_call_target="tpu_custom_call" | custom-call | tf_op jit(solution)/shard_map/prepare/pallas_call | solution.py:346
  2.3 0.0 copy-done
  2.3 45.3 %conditional.1 = (f32[12,96]{1,0:T(8,128)S(1)}) conditional(s32[]{:T(128)} %bitcast.3, (f32[16,128]{1,0:T(8,128)S(1)}, s32[128,128]{1,0:T(8,128)S(1)}) %tuple.46, (f32[16,128]{1,0:T(8,128)S(1)}, s32[128,128]{1,0:T(8,128)S(1)}) %tuple.47, (f32[16,128]{1,0:T(8,128)S(1)}, s32[128,128]{1,0:T(8,128)S(1)}) %tuple.48, ...), branch_computations={%region_0.0_spmd, %region_1.0_spmd, %region_2.0_spmd, %region_3.0_... | conditional | bytes 8 | solution.py:357
  2.4 44.7 %step_11.1 = f32[12,96]{1,0:T(8,128)S(1)} custom-call(f32[16,128]{1,0:T(8,128)S(1)} %get-tuple-element.43.state_hbm, s32[128,128]{1,0:T(8,128)S(1)} %get-tuple-element.44.active_hbm), custom_call_target="tpu_custom_call" | custom-call | tf_op jit(solution)/shard_map/cond/branch_1_fun/step_11/pallas_call | solution.py:357
  47.7 0.6 %copy.22 = f32[12,96]{1,0:T(8,128)} copy(f32[12,96]{1,0:T(8,128)S(1)} %get-tuple-element.66) | data formatting | bytes 9216
Async XLA Ops:
  0.0 2.3 %copy-start = (s32[16384]{0:T(1024)S(1)}, s32[16384]{0:T(1024)}, u32[]{:S(2)}) copy-start(s32[16384]{0:T(1024)} %param.15) | copy-start | bytes 196612

commit v3 on v2

--- a/solution.py
+++ b/solution.py
@@ -13,11 +13,7 @@
 GROUP = 32
 RING = 16
 REACH = 4
-UNROLL = 32
-NEAR = (-4, 4, -3, 3, -2, 2, -1, 1)
-EARLY = (0, 1, 15, 2, 14, 3, 13, 4)
-HALF = RING * LANES // (16 * UNROLL)
-LATE = (12, 5, 6, 7, 8, 9, 10, 11)
+CHUNK = 128
 ROWS = 6
 SOFT = 0.01
 BLOCK_COUNTS = (10, 11, 12, 13, 14, 16, 20, 24)
@@ -39,24 +35,26 @@
     )
 
 
-def pull(targets, sources, acc):
+def halves(x):
+    high = x.astype(jnp.bfloat16)
+    return high, (x - high.astype(jnp.float32)).astype(jnp.bfloat16)
+
+
+def strengths(targets, sources):
     sep = [sources[d] - targets[d] for d in range(3)]
     rel = [sources[3 + d] - targets[3 + d] for d in range(3)]
     dist_sq = (sep[0] * sep[0] + SOFT) + sep[1] * sep[1] + sep[2] * sep[2]
     inverse = lax.rsqrt(dist_sq)
     inverse_sq = inverse * inverse
-    strength = (sources[6] * inverse) * inverse_sq
+    strength = inverse * inverse_sq
     radial = sep[0] * rel[0] + sep[1] * rel[1] + sep[2] * rel[2]
     turned = (radial * inverse_sq) * strength
-    accel = [acc[d] + strength * sep[d] for d in range(3)]
-    swing = [acc[3 + d] + strength * rel[d] for d in range(3)]
-    drag = [acc[6 + d] + turned * sep[d] for d in range(3)]
-    return accel + swing + drag
+    return [jnp.concatenate(pair, axis=1) for pair in zip(halves(strength), halves(turned))]
 
 
 def kernel(
     blocks, state_hbm, active_hbm, out_ref, state, active_ref,
-    old, tbuf, zbuf, spread, tgt, offs, accs, fresh, rout, rin,
+    old, tbuf, zbuf, spread, weigh, middle, pend, tgt, offs, accs, fresh, rout, rin,
     load, tsend, trecv, zsend, zrecv, fsend, frecv, rsend, rrecv,
 ):
     wide = lax.axis_index("wide")
@@ -82,8 +80,19 @@
         pl.semaphore_signal(barrier, inc=1, device_id=mate(i)[1], device_id_type=MESH)
         return carry
 
-    for shift in NEAR:
-        pl.semaphore_signal(barrier, inc=1, device_id=along(shift), device_id_type=MESH)
+    quarter = level // 4
+    odd = quarter % 2
+    upper = level // 8
+    inward = 1 - 2 * odd
+    edge = level % 4 + odd * (3 - 2 * (level % 4))
+
+    for k in range(1, REACH + 1):
+        pl.semaphore_signal(barrier, inc=1, device_id=along(inward * k), device_id_type=MESH)
+
+        @pl.when((edge >= k) | (upper == 0))
+        def _():
+            pl.semaphore_signal(barrier, inc=1, device_id=along(-inward * k), device_id_type=MESH)
+
     lax.fori_loop(1, GROUP, greet, 0)
 
     loads = [
@@ -139,7 +148,7 @@
     chosen = jnp.where(lane == LANES - 1, count.astype(jnp.float32), chosen)
     tbuf[member] = chosen
 
-    pl.semaphore_wait(barrier, GROUP - 1 + len(NEAR))
+    pl.semaphore_wait(barrier, GROUP - 1 + REACH + edge + upper * (REACH - edge))
 
     def send_target(i, carry):
         pltpu.make_async_remote_copy(
@@ -148,39 +157,73 @@
         ).start()
         return carry
 
-    for shift in NEAR:
+    def send_source(shift):
+        slot = (RING - shift) % RING
         pltpu.make_async_remote_copy(
-            src_ref=zbuf.at[0], dst_ref=zbuf.at[(RING - shift) % RING],
-            send_sem=zsend, recv_sem=zrecv, device_id=along(shift), device_id_type=MESH,
+            src_ref=zbuf.at[0], dst_ref=zbuf.at[slot],
+            send_sem=zsend, recv_sem=zrecv.at[slot], device_id=along(shift), device_id_type=MESH,
         ).start()
+
+    def await_source(shift):
+        slot = (RING + shift) % RING
+        tile = zbuf.at[slot]
+        pltpu.make_async_copy(tile, tile, zrecv.at[slot]).wait()
+
+    for k in range(REACH, 0, -1):
+        send_source(inward * k)
+
+        @pl.when((edge >= k) | (upper == 1))
+        def _():
+            send_source(-inward * k)
+
     lax.fori_loop(1, GROUP, send_target, 0)
 
     old[0:8, :] = lane_gather(state[0:8, :], picked)
     old[8:16, :] = lane_gather(state[8:16, :], picked)
 
+    mean = jnp.sum(zbuf[0], axis=1, keepdims=True) * (1.0 / LANES)
+    middle[...] = jnp.where(sub < 6, jnp.broadcast_to(mean, (8, LANES)), 0.0)
+
     def spread_tile(slot, place):
-        turned = zbuf[slot].T
-        for d in range(7):
-            spread[d, place * LANES : (place + 1) * LANES, :] = jnp.broadcast_to(
-                turned[:, d : d + 1], (LANES, LANES)
-            )
+        tile = zbuf[slot]
+        turned = tile.T
+        lanes = slice(place * LANES, (place + 1) * LANES)
+        for d in range(6):
+            spread[d, lanes, :] = jnp.broadcast_to(turned[:, d : d + 1], (LANES, LANES))
+        mass = rows8(tile[6:7, :])
+        rest = jnp.where(sub < 6, (tile - middle[...]) * mass, jnp.where(sub == 6, mass, 0.0))
+        pieces = []
+        for _ in range(3):
+            pieces.append(rest.astype(jnp.bfloat16).astype(jnp.float32))
+            rest = rest - pieces[-1]
+        pieces.append(jnp.zeros((8, LANES), jnp.float32))
+        weigh[:, lanes] = jnp.concatenate(pieces, axis=0).astype(jnp.bfloat16)
 
     spread_tile(0, 0)
 
-    direct = zbuf.at[pl.ds(0, len(NEAR))]
-    passed = zbuf.at[pl.ds(0, RING - 1 - len(NEAR))]
-    pltpu.make_async_copy(direct, direct, zrecv).wait()
-    pltpu.make_async_remote_copy(
-        src_ref=zbuf.at[pl.ds(1, REACH)], dst_ref=zbuf.at[pl.ds(1 + REACH, REACH)],
-        send_sem=fsend, recv_sem=frecv, device_id=along(-REACH), device_id_type=MESH,
-    ).start()
-    pltpu.make_async_remote_copy(
-        src_ref=zbuf.at[pl.ds(RING - REACH + 1, REACH - 1)],
-        dst_ref=zbuf.at[pl.ds(RING - 2 * REACH + 1, REACH - 1)],
-        send_sem=fsend, recv_sem=frecv, device_id=along(REACH), device_id_type=MESH,
-    ).start()
-    for place, slot in enumerate(EARLY[1:]):
-        spread_tile(slot, 1 + place)
+    direct = zbuf.at[pl.ds(0, 2 * REACH)]
+    passed = zbuf.at[pl.ds(0, RING - 1 - 2 * REACH)]
+
+    def settle():
+        for k in range(1, REACH + 1):
+            await_source(-inward * k)
+
+            @pl.when((edge < k) & (upper == 0))
+            def _():
+                send_source(-inward * k)
+
+    def pass_up():
+        pltpu.make_async_remote_copy(
+            src_ref=zbuf.at[pl.ds(RING - REACH + 1, REACH - 1)],
+            dst_ref=zbuf.at[pl.ds(RING - 2 * REACH + 1, REACH - 1)],
+            send_sem=fsend, recv_sem=frecv, device_id=along(REACH), device_id_type=MESH,
+        ).start()
+
+    def pass_down():
+        pltpu.make_async_remote_copy(
+            src_ref=zbuf.at[pl.ds(1, REACH)], dst_ref=zbuf.at[pl.ds(1 + REACH, REACH)],
+            send_sem=fsend, recv_sem=frecv, device_id=along(-REACH), device_id_type=MESH,
+        ).start()
 
     others = tbuf.at[pl.ds(0, GROUP - 1), pl.ds(0, ROWS)]
     pltpu.make_async_copy(others, others, trecv).wait()
@@ -205,39 +248,100 @@
     for b in range(blocks):
         tgt[b] = laid[1 + b]
 
-    def pairs(b, acc, first, chunks):
-        targets = [rows8(tgt[b, d : d + 1, :]) for d in range(6)]
-
-        def chunk(k, acc):
-            acc = list(acc)
-            for u in range(UNROLL):
-                place = pl.ds(pl.multiple_of((first + k) * (8 * UNROLL) + 8 * u, 8), 8)
-                acc = pull(targets, [spread[d, place, :] for d in range(7)], acc)
-            return tuple(acc)
-
-        return lax.fori_loop(0, chunks, chunk, acc)
-
-    def near(b, carry):
-        acc = pairs(b, (jnp.zeros((8, LANES), jnp.float32),) * 9, 0, HALF)
-        for d in range(9):
-            accs[b, d] = acc[d]
-        return carry
-
-    lax.fori_loop(0, blocks, near, 0)
+    for k in range(1, REACH + 1):
+        await_source(inward * k)
+
+    @pl.when(quarter == 1)
+    def _():
+        settle()
+        pass_up()
+        pass_down()
+
+    @pl.when(quarter == 2)
+    def _():
+        pass_down()
+
+    @pl.when(quarter == 3)
+    def _():
+        pass_up()
+
+    for k in range(1, REACH + 1):
+        spread_tile((RING + inward * k) % RING, k)
+
+    def work(first_tile, tiles):
+        begin_row, end_row = first_tile * LANES, (first_tile + tiles) * LANES
+
+        def product(lanes, piece):
+            return jnp.dot(weigh[:, lanes], piece, preferred_element_type=jnp.float32)
+
+        last = slice(end_row - CHUNK, end_row)
+
+        def left():
+            return product(last, pend[0]) + product(last, pend[1])
+
+        def block(b, carry):
+            late = left()
+            targets = [
+                jnp.broadcast_to(tgt[b, d : d + 1, :], (16, LANES)) for d in range(6)
+            ]
+            acc = jnp.zeros((32, 2 * LANES), jnp.float32)
+            for first in range(begin_row, end_row, CHUNK):
+                parts = [
+                    strengths(targets, [spread[d, row : row + 16, :] for d in range(6)])
+                    for row in range(first, first + CHUNK, 16)
+                ]
+                for p in range(2):
+                    piece = jnp.concatenate([part[p] for part in parts], axis=0)
+                    if first + CHUNK < end_row:
+                        acc = acc + product(slice(first, first + CHUNK), piece)
+                    else:
+                        pend[p] = piece
+            accs[b] = accs[b] + late
+            accs[b + 1] = accs[b + 1] + acc
+            return carry
+
+        pend[...] = jnp.zeros_like(pend)
+        lax.fori_loop(0, blocks, block, 0)
+        accs[blocks] = accs[blocks] + left()
+
+    accs[...] = jnp.zeros_like(accs)
+    work(0, 1 + REACH)
+
+    @pl.when(quarter == 0)
+    def _():
+        settle()
+        pass_up()
+        pass_down()
+
+    @pl.when(quarter == 2)
+    def _():
+        settle()
+        pass_up()
+
+    @pl.when(quarter == 3)
+    def _():
+        settle()
+        pass_down()
+
+    for k in range(1, REACH + 1):
+        spread_tile((RING - inward * k) % RING, REACH + k)
+    work(1 + REACH, REACH)
 
     pltpu.make_async_copy(passed, passed, frecv).wait()
-    for place, slot in enumerate(LATE):
-        spread_tile(slot, len(EARLY) + place)
-
-    def far(b, carry):
-        acc = pairs(b, tuple(accs[b, d] for d in range(9)), HALF, HALF)
-        for d in range(3):
-            fresh[b, d : d + 1, :] = jnp.sum(acc[d], axis=0, keepdims=True)
-            fresh[b, 3 + d : 4 + d, :] = jnp.sum(acc[3 + d] - 3.0 * acc[6 + d], axis=0, keepdims=True)
+    for slot in range(REACH + 1, RING - REACH):
+        spread_tile(slot, REACH + slot)
+    work(1 + 2 * REACH, RING - 1 - 2 * REACH)
+
+    for b in range(blocks):
+        acc = accs[b + 1]
+        acc = acc[0:8] + acc[8:16] + acc[16:24]
+        drawn, dragged = acc[:, :LANES], acc[:, LANES:]
+        here = tgt[b] - middle[...]
+        pulled = drawn - here * rows8(drawn[6:7, :])
+        slowed = dragged - here * rows8(dragged[6:7, :])
+        fresh[b, 0:6, :] = pulled[0:6, :]
+        fresh[b, 3:6, :] = pulled[3:6, :] - 3.0 * slowed[0:3, :]
         fresh[b, 6:8, :] = jnp.zeros((2, LANES), jnp.float32)
-        return carry
-
-    lax.fori_loop(0, blocks, far, 0)
 
     def cut(o):
         off = offs[o]
@@ -326,16 +430,19 @@
                 pltpu.VMEM((16, LANES), jnp.float32),
                 pltpu.VMEM((GROUP, *tile), jnp.float32),
                 pltpu.VMEM((RING, *tile), jnp.float32),
-                pltpu.VMEM((7, RING * LANES, LANES), jnp.float32),
+                pltpu.VMEM((6, RING * LANES, LANES), jnp.float32),
+                pltpu.VMEM((32, RING * LANES), jnp.bfloat16),
+                pltpu.VMEM(tile, jnp.float32),
+                pltpu.VMEM((2, CHUNK, 2 * LANES), jnp.bfloat16),
                 pltpu.VMEM((blocks, *tile), jnp.float32),
                 pltpu.VMEM((GROUP, *tile), jnp.int32),
-                pltpu.VMEM((blocks, 9, *tile), jnp.float32),
+                pltpu.VMEM((blocks + 1, 32, 2 * LANES), jnp.float32),
                 pltpu.VMEM((blocks, *tile), jnp.float32),
                 pltpu.VMEM((GROUP, *tile), jnp.float32),
                 pltpu.VMEM((GROUP, *tile), jnp.float32),
-                dma((2,)),
+                dma((2,)), dma(()), dma(()), dma(()), dma((RING,)),
             ]
-            + [dma(())] * 8,
+            + [dma(())] * 4,
             compiler_params=pltpu.CompilerParams(
                 collective_id=which, has_side_effects=True, vmem_limit_bytes=40 << 20
             ),

time: 48.4 us -> 45.3 us (0.936)
  Pallas kernels: 46.4 us -> 43.2 us
    pallas_call x1, Pallas kernels: 44.7 us -> 41.6 us  [on_device(): lax.switch(which[0], [branch(i, b) for i, b in enumerate(BLOCK_COUNTS)],...]
where the time goes in v3:
time: 45.3 us; the launch traced here: 45.2 us
  Pallas kernels  43.2 us (95%)
  between operations  0.67 us (1%)
  loops' own time  0.65 us (1%)
  local copies, waits for them, and re-layouts  0.6 us (1%)
    pallas_call x1, Pallas kernels, on_device(): lax.switch(which[0], [branch(i, b) for i, b in enumerate(BLOCK_COUNTS)],...  41.6 us
    pallas_call x1, Pallas kernels, on_device(): pl.pallas_call(functools.partial(prepare, grav), out_shape=(jax.ShapeDtyp...  1.68 us

profile of v3, /device:TPU:1, one launch (start us, length us, event | category | flops | bytes accessed | tf_op | source)
XLA Modules:
  0.0 45.2 jit_solution(12349544050240999533)
XLA Ops:
  0.0 0.0 copy-start
  0.0 1.7 %prepare.1 = (s32[1]{0:T(128)}, f32[16,128]{1,0:T(8,128)S(1)}) custom-call(s32[128,128]{1,0:T(8,128)} %bitcast.4, f32[12,128]{1,0:T(8,128)} %star_ref.1, f32[1,128]{1,0:T(1,128)} %bitcast.13, s32[1,128]{1,0:T(1,128)} %bitcast.14), custom_call_target="tpu_custom_call" | custom-call | tf_op jit(solution)/shard_map/prepare/pallas_call | solution.py:453
  2.3 0.0 copy-done
  2.3 42.2 %conditional.1 = (f32[12,96]{1,0:T(8,128)S(1)}) conditional(s32[]{:T(128)} %bitcast.3, (f32[16,128]{1,0:T(8,128)S(1)}, s32[128,128]{1,0:T(8,128)S(1)}) %tuple.46, (f32[16,128]{1,0:T(8,128)S(1)}, s32[128,128]{1,0:T(8,128)S(1)}) %tuple.47, (f32[16,128]{1,0:T(8,128)S(1)}, s32[128,128]{1,0:T(8,128)S(1)}) %tuple.48, ...), branch_computations={%region_0.0_spmd, %region_1.0_spmd, %region_2.0_spmd, %region_3.0_... | conditional | bytes 8 | solution.py:464
  2.4 41.6 %step_11.1 = f32[12,96]{1,0:T(8,128)S(1)} custom-call(f32[16,128]{1,0:T(8,128)S(1)} %get-tuple-element.43.state_hbm, s32[128,128]{1,0:T(8,128)S(1)} %get-tuple-element.44.active_hbm), custom_call_target="tpu_custom_call" | custom-call | tf_op jit(solution)/shard_map/cond/branch_1_fun/step_11/pallas_call | solution.py:464
  44.6 0.6 %copy.22 = f32[12,96]{1,0:T(8,128)} copy(f32[12,96]{1,0:T(8,128)S(1)} %get-tuple-element.66) | data formatting | bytes 9216
Async XLA Ops:
  0.0 2.3 %copy-start = (s32[16384]{0:T(1024)S(1)}, s32[16384]{0:T(1024)}, u32[]{:S(2)}) copy-start(s32[16384]{0:T(1024)} %param.15) | copy-start | bytes 196612

commit v4 on v3

--- a/solution.py
+++ b/solution.py
@@ -280,7 +280,6 @@
             return product(last, pend[0]) + product(last, pend[1])
 
         def block(b, carry):
-            late = left()
             targets = [
                 jnp.broadcast_to(tgt[b, d : d + 1, :], (16, LANES)) for d in range(6)
             ]
@@ -292,17 +291,14 @@
                 ]
                 for p in range(2):
                     piece = jnp.concatenate([part[p] for part in parts], axis=0)
-                    if first + CHUNK < end_row:
+                    if True:
                         acc = acc + product(slice(first, first + CHUNK), piece)
                     else:
                         pend[p] = piece
-            accs[b] = accs[b] + late
             accs[b + 1] = accs[b + 1] + acc
             return carry
 
-        pend[...] = jnp.zeros_like(pend)
         lax.fori_loop(0, blocks, block, 0)
-        accs[blocks] = accs[blocks] + left()
 
     accs[...] = jnp.zeros_like(accs)
     work(0, 1 + REACH)

time: 45.3 us -> 45.6 us (level); the launches traced: 45.2 us -> 46.2 us
  Pallas kernels: 43.2 us -> 44.2 us
    pallas_call x1, Pallas kernels: 41.6 us -> 42.5 us  [on_device(): lax.switch(which[0], [branch(i, b) for i, b in enumerate(BLOCK_COUNTS)],...]
where the time goes in v4:
time: 45.6 us; the launch traced here: 46.2 us
  Pallas kernels  44.2 us (97%)
  loops' own time  0.75 us (2%)
  between operations  0.67 us (1%)
  local copies, waits for them, and re-layouts  0.6 us (1%)
    pallas_call x1, Pallas kernels, on_device(): lax.switch(which[0], [branch(i, b) for i, b in enumerate(BLOCK_COUNTS)],...  42.5 us
    pallas_call x1, Pallas kernels, on_device(): pl.pallas_call(functools.partial(prepare, grav), out_shape=(jax.ShapeDtyp...  1.68 us

profile of v4, /device:TPU:1, one launch (start us, length us, event | category | flops | bytes accessed | tf_op | source)
XLA Modules:
  0.0 46.2 jit_solution(15728309727672115951)
XLA Ops:
  0.0 0.0 copy-start
  0.0 1.7 %prepare.1 = (s32[1]{0:T(128)}, f32[16,128]{1,0:T(8,128)S(1)}) custom-call(s32[128,128]{1,0:T(8,128)} %bitcast.4, f32[12,128]{1,0:T(8,128)} %star_ref.1, f32[1,128]{1,0:T(1,128)} %bitcast.13, s32[1,128]{1,0:T(1,128)} %bitcast.14), custom_call_target="tpu_custom_call" | custom-call | tf_op jit(solution)/shard_map/prepare/pallas_call | solution.py:449
  2.3 0.0 copy-done
  2.3 43.2 %conditional.1 = (f32[12,96]{1,0:T(8,128)S(1)}) conditional(s32[]{:T(128)} %bitcast.3, (f32[16,128]{1,0:T(8,128)S(1)}, s32[128,128]{1,0:T(8,128)S(1)}) %tuple.46, (f32[16,128]{1,0:T(8,128)S(1)}, s32[128,128]{1,0:T(8,128)S(1)}) %tuple.47, (f32[16,128]{1,0:T(8,128)S(1)}, s32[128,128]{1,0:T(8,128)S(1)}) %tuple.48, ...), branch_computations={%region_0.0_spmd, %region_1.0_spmd, %region_2.0_spmd, %region_3.0_... | conditional | bytes 8 | solution.py:460
  2.4 42.5 %step_12.1 = f32[12,96]{1,0:T(8,128)S(1)} custom-call(f32[16,128]{1,0:T(8,128)S(1)} %get-tuple-element.48.state_hbm, s32[128,128]{1,0:T(8,128)S(1)} %get-tuple-element.50.active_hbm), custom_call_target="tpu_custom_call" | custom-call | tf_op jit(solution)/shard_map/cond/branch_2_fun/step_12/pallas_call | solution.py:460
  45.6 0.6 %copy.22 = f32[12,96]{1,0:T(8,128)} copy(f32[12,96]{1,0:T(8,128)S(1)} %get-tuple-element.66) | data formatting | bytes 9216
Async XLA Ops:
  0.0 2.3 %copy-start = (s32[16384]{0:T(1024)S(1)}, s32[16384]{0:T(1024)}, u32[]{:S(2)}) copy-start(s32[16384]{0:T(1024)} %param.15) | copy-start | bytes 196612
